TPU v7x, 32 devices: a whole 2x2x4 slice. The times are simulated.
32 devices in a mesh: dp: 8 (over z, y), tp: 4 (over x, core).
Axes of the slice: x: 2, y: 2, z: 4, core: 2. Of those that a mesh axis runs over, the one named last changes fastest.
Arguments:
- inputs: bfloat16 [32, 896, 512], P('dp', 'tp'), may hold values from -6 to 6
- dataset: int32 [32], P('dp'), may hold values from 0 to 3, as said below
- variate_mask: int32 [32, 896], P('dp'), may hold values from 0 to 1, as said below
- dataset_bias: bfloat16 [4, 512], replicated, may hold values from -3 to 3
- w_qkv: bfloat16 [3, 512, 512], P(None, None, 'tp'), may hold values from -0.25 to 0.25
- qv_bias: bfloat16 [2, 512], P(None, 'tp'), may hold values from -1.796875 to 1.796875
- w_out: bfloat16 [512, 512], P('tp'), may hold values from -1 to 1
- out_bias: bfloat16 [2, 512], replicated, may hold values from -1.796875 to 1.796875
- w_up: bfloat16 [512, 2048], P(None, 'tp'), may hold values from -0.25 to 0.25
- up_bias: bfloat16 [2048], P('tp'), may hold values from -1.796875 to 1.796875
- w_down: bfloat16 [2048, 512], P('tp'), may hold values from -0.125 to 0.125
- norm_gain: bfloat16 [2, 512], replicated, may hold values from 0.25 to 1.75
- norm_shift: bfloat16 [2, 512], replicated, may hold values from -1.796875 to 1.796875
- cotangent: bfloat16 [32, 896, 512], P('dp', 'tp'), may hold values from -6 to 6
Outputs:
- outputs: bfloat16 [32, 896, 512], P('dp', 'tp')
- input_grad: bfloat16 [32, 896, 512], P('dp', 'tp')
- dataset_bias_grad: float32 [4, 512], replicated
- w_qkv_grad: float32 [3, 512, 512], P(None, None, 'tp')
- qv_bias_grad: float32 [2, 512], P(None, 'tp')
- w_out_grad: float32 [512, 512], P('tp')
- out_bias_grad: float32 [2, 512], replicated
- w_up_grad: float32 [512, 2048], P(None, 'tp')
- up_bias_grad: float32 [2048], P('tp')
- w_down_grad: float32 [2048, 512], P('tp')
- norm_gain_grad: float32 [2, 512], replicated
- norm_shift_grad: float32 [2, 512], replicated
Inputs may be any that keep to these rules, and one draw needn't show every extreme that they name: In every aligned block of 4 windows (those of one index of dp) at least one window has dataset 3. `variate_mask`: variate 0 of every window is live. A window of dataset c has no live variate at or past entry c of (max(1, 7), max(1, 21), max(1, 321), max(1, 862)).
All inputs are finite; a program needn't handle non-finite values.
Results may differ from a plain program's by a relative error of at most 0.017.
Values may be sent and summed in bfloat16 or wider, within the bound.
A program may use at most 128 MiB of HBM per device.

v0:
```python
import math
import jax
import jax.numpy as jnp
from jax import lax
from jax.sharding import PartitionSpec as P

HD = 64
EPSILON = 1e-05
HIGHEST = lax.Precision.HIGHEST
NEG_FILL = -1e30


def layer_forward_norm(residual, gains, shifts):
    center = residual - jnp.mean(residual, axis=-1, keepdims=True)
    factor = lax.rsqrt(jnp.mean(center * center, axis=-1, keepdims=True) + EPSILON)
    normed = center * factor
    return (normed * gains + shifts, normed, factor)


def layer_back_norm(upstream, normed, factor, gains):
    scaled = upstream * gains
    result = factor * (
        scaled
        - jnp.mean(scaled, axis=-1, keepdims=True)
        - normed * jnp.mean(scaled * normed, axis=-1, keepdims=True)
    )
    return (result, jnp.sum(upstream * normed, axis=(0, 1)), jnp.sum(upstream, axis=(0, 1)))


def masked_scores(queries, key_rows, live_row):
    length = queries.shape[0]
    head_count = queries.shape[1] // HD
    q_heads = queries.reshape(length, head_count, HD)
    k_heads = key_rows.reshape(length, head_count, HD)
    scores = jnp.einsum("qhe,khe->hqk", q_heads, k_heads, preferred_element_type=jnp.float32) * (
        1.0 / math.sqrt(HD)
    )
    return (jnp.where(live_row[None, None, :] > 0.5, scores, NEG_FILL), q_heads, k_heads)


def attend_window(packed):
    queries, key_rows, value_rows, live_row = packed
    length = queries.shape[0]
    head_count = queries.shape[1] // HD
    scores, q_heads, k_heads = masked_scores(queries, key_rows, live_row)
    row_top = jnp.max(scores, axis=-1, keepdims=True)
    exponent = jnp.exp(scores - row_top)
    row_total = jnp.sum(exponent, axis=-1, keepdims=True)
    attn_prob = (exponent / row_total).astype(jnp.bfloat16)
    v_heads = value_rows.reshape(length, head_count, HD)
    mixture = jnp.einsum("hqk,khe->qhe", attn_prob, v_heads, preferred_element_type=jnp.float32)
    log_total = (row_top + jnp.log(row_total))[..., 0]
    return (mixture.reshape(length, head_count * HD).astype(jnp.bfloat16), log_total)


def attend_back(packed):
    queries, key_rows, value_rows, live_row, grad_out, log_total = packed
    length = queries.shape[0]
    head_count = queries.shape[1] // HD
    scores, q_heads, k_heads = masked_scores(queries, key_rows, live_row)
    attn_prob = jnp.exp(scores - log_total[..., None])
    prob_low = attn_prob.astype(jnp.bfloat16)
    v_heads = value_rows.reshape(length, head_count, HD)
    grad_heads = grad_out.reshape(length, head_count, HD)
    grad_values = jnp.einsum(
        "hqk,qhe->khe", prob_low, grad_heads, preferred_element_type=jnp.float32
    )
    grad_probs = jnp.einsum("qhe,khe->hqk", grad_heads, v_heads, preferred_element_type=jnp.float32)
    grad_scores = attn_prob * (grad_probs - jnp.sum(attn_prob * grad_probs, axis=-1, keepdims=True))
    score_low = grad_scores.astype(jnp.bfloat16)
    score_scale = 1.0 / math.sqrt(HD)
    grad_queries = (
        jnp.einsum("hqk,khe->qhe", score_low, k_heads, preferred_element_type=jnp.float32)
        * score_scale
    )
    grad_keys = (
        jnp.einsum("hqk,qhe->khe", score_low, q_heads, preferred_element_type=jnp.float32)
        * score_scale
    )
    joined = jnp.concatenate(
        [
            grad_queries.reshape(length, head_count * HD),
            grad_keys.reshape(length, head_count * HD),
            grad_values.reshape(length, head_count * HD),
        ],
        axis=-1,
    )
    return joined.astype(jnp.bfloat16)


def attention_forward(gathered, w_cat, b_cat, w_out, live_full):
    projected = (
        jnp.einsum("wvd,de->wve", gathered, w_cat, preferred_element_type=jnp.float32) + b_cat
    ).astype(jnp.bfloat16)
    col_width = w_out.shape[0]
    mixture, log_total = lax.map(
        attend_window,
        (
            projected[..., :col_width],
            projected[..., col_width : 2 * col_width],
            projected[..., 2 * col_width :],
            live_full,
        ),
    )
    part_sum = jnp.einsum("wvh,hd->wvd", mixture, w_out, preferred_element_type=jnp.float32)
    return (part_sum, projected, mixture, log_total)


def attention_back(grad_rows, gathered, projected, mixture, log_total, live_full, w_cat, w_out):
    w_out_g = jnp.einsum("wvh,wvd->hd", mixture, grad_rows, preferred_element_type=jnp.float32)
    grad_mixture = jnp.einsum(
        "wvd,hd->wvh", grad_rows, w_out, preferred_element_type=jnp.float32
    ).astype(jnp.bfloat16)
    col_width = w_out.shape[0]
    grad_proj = lax.map(
        attend_back,
        (
            projected[..., :col_width],
            projected[..., col_width : 2 * col_width],
            projected[..., 2 * col_width :],
            live_full,
            grad_mixture,
            log_total,
        ),
    )
    w_cat_g = jnp.einsum("wvd,wve->de", gathered, grad_proj, preferred_element_type=jnp.float32)
    b_cat_g = jnp.sum(grad_proj, axis=(0, 1), dtype=jnp.float32)
    part_sum = jnp.einsum("wve,de->wvd", grad_proj, w_cat, preferred_element_type=jnp.float32)
    return (part_sum, w_cat_g, b_cat_g, w_out_g)


def feed_forward(gathered, w_up, up_bias, w_down):
    pre_act = jnp.einsum(
        "wvd,df->wvf", gathered, w_up, preferred_element_type=jnp.float32
    ) + up_bias.astype(jnp.float32)
    act_full, gelu_back = jax.vjp(jax.nn.gelu, pre_act)
    act_low = act_full.astype(jnp.bfloat16)
    part_sum = jnp.einsum("wvf,fd->wvd", act_low, w_down, preferred_element_type=jnp.float32)
    return (part_sum, act_low, gelu_back)


def feed_back(grad_rows, gathered, act_low, gelu_back, w_up, w_down):
    w_down_g = jnp.einsum("wvf,wvd->fd", act_low, grad_rows, preferred_element_type=jnp.float32)
    grad_act = jnp.einsum("wvd,fd->wvf", grad_rows, w_down, preferred_element_type=jnp.float32)
    grad_pre = gelu_back(grad_act)[0]
    up_bias_g = jnp.sum(grad_pre, axis=(0, 1))
    grad_low = grad_pre.astype(jnp.bfloat16)
    w_up_g = jnp.einsum("wvd,wvf->df", gathered, grad_low, preferred_element_type=jnp.float32)
    part_sum = jnp.einsum("wvf,df->wvd", grad_low, w_up, preferred_element_type=jnp.float32)
    return (part_sum, w_up_g, up_bias_g, w_down_g)


def shards(
    inputs,
    dataset,
    variate_mask,
    dataset_bias,
    w_qkv,
    qv_bias,
    w_out,
    out_bias,
    w_up,
    up_bias,
    w_down,
    norm_gain,
    norm_shift,
    cotangent,
):
    my_rank = lax.axis_index("tp")
    one_hot = (
        dataset[:, None] == jnp.arange(dataset_bias.shape[0], dtype=jnp.int32)[None, :]
    ).astype(jnp.float32)
    offsets = jnp.dot(one_hot, dataset_bias.astype(jnp.float32), precision=HIGHEST)
    gains = norm_gain.astype(jnp.float32)
    shifts = norm_shift.astype(jnp.float32)
    biases = out_bias.astype(jnp.float32)
    rows_in, cot_in = (inputs, cotangent)
    qkv_used, qvb_used, out_used, up_used, upb_used, down_used = (
        w_qkv,
        qv_bias,
        w_out,
        w_up,
        up_bias,
        w_down,
    )
    row_start = my_rank * inputs.shape[1]
    row_span = rows_in.shape[1]
    win_live = variate_mask.astype(jnp.float32)
    live_rows = lax.dynamic_slice_in_dim(win_live, row_start, row_span, 1)
    col_width = out_used.shape[0]
    model_width = qkv_used.shape[1]
    w_cat = jnp.transpose(qkv_used, (1, 0, 2)).reshape(model_width, 3 * col_width)
    b_cat = jnp.concatenate(
        [
            qvb_used[0].astype(jnp.float32),
            jnp.zeros((col_width,), jnp.float32),
            qvb_used[1].astype(jnp.float32),
        ]
    )
    base_rows = rows_in.astype(jnp.float32) + offsets[:, None, :]
    act_in = base_rows.astype(jnp.bfloat16)
    act_full = lax.all_gather(act_in, "tp", axis=1, tiled=True)
    attn_part, projected, mixture, log_total = attention_forward(
        act_full, w_cat, b_cat, out_used, win_live
    )
    attn_sum = lax.psum_scatter(attn_part, "tp", scatter_dimension=1, tiled=True)
    hidden, normed_one, factor_one = layer_forward_norm(
        base_rows + attn_sum + biases[0], gains[0], shifts[0]
    )
    hidden_low = hidden.astype(jnp.bfloat16)
    hidden_full = lax.all_gather(hidden_low, "tp", axis=1, tiled=True)
    ffn_part, act_low, gelu_back = feed_forward(hidden_full, up_used, upb_used, down_used)
    ffn_sum = lax.psum_scatter(
        ffn_part.astype(jnp.bfloat16), "tp", scatter_dimension=1, tiled=True
    ).astype(jnp.float32)
    final_rows, normed_two, factor_two = layer_forward_norm(
        hidden + ffn_sum + biases[1], gains[1], shifts[1]
    )
    result_rows = (final_rows * live_rows[:, :, None]).astype(jnp.bfloat16)
    grad_final = cot_in.astype(jnp.float32) * live_rows[:, :, None]
    grad_two, gain_two, shift_two = layer_back_norm(grad_final, normed_two, factor_two, gains[1])
    grad_two_low = grad_two.astype(jnp.bfloat16)
    grad_two_full = lax.all_gather(grad_two_low, "tp", axis=1, tiled=True)
    ffn_back_part, up_grad, upb_grad, down_grad = feed_back(
        grad_two_full, hidden_full, act_low, gelu_back, up_used, down_used
    )
    ffn_back = lax.psum_scatter(
        ffn_back_part.astype(jnp.bfloat16), "tp", scatter_dimension=1, tiled=True
    ).astype(jnp.float32)
    grad_one, gain_one, shift_one = layer_back_norm(
        grad_two + ffn_back, normed_one, factor_one, gains[0]
    )
    grad_one_low = grad_one.astype(jnp.bfloat16)
    grad_one_full = lax.all_gather(grad_one_low, "tp", axis=1, tiled=True)
    attn_back_part, cat_grad, bcat_grad, out_grad = attention_back(
        grad_one_full, act_full, projected, mixture, log_total, win_live, w_cat, out_used
    )
    attn_back = lax.psum_scatter(
        attn_back_part.astype(jnp.bfloat16), "tp", scatter_dimension=1, tiled=True
    ).astype(jnp.float32)
    grad_base = grad_one + attn_back
    input_low = grad_base.astype(jnp.bfloat16)
    bias_grad = jnp.dot(one_hot.T, jnp.sum(grad_base, axis=1), precision=HIGHEST)
    qkv_grad = jnp.transpose(cat_grad.reshape(model_width, 3, col_width), (1, 0, 2))
    qvb_grad = jnp.stack([bcat_grad[:col_width], bcat_grad[2 * col_width :]])
    weight_totals = lax.psum((qkv_grad, qvb_grad, out_grad, up_grad, upb_grad, down_grad), "dp")
    shared = lax.psum(
        (
            bias_grad,
            jnp.stack([gain_one, gain_two]),
            jnp.stack([shift_one, shift_two]),
            jnp.stack([jnp.sum(grad_one, axis=(0, 1)), jnp.sum(grad_two, axis=(0, 1))]),
        ),
        ("dp", "tp"),
    )
    return (
        result_rows,
        input_low,
        shared[0],
        weight_totals[0],
        weight_totals[1],
        weight_totals[2],
        shared[3],
        weight_totals[3],
        weight_totals[4],
        weight_totals[5],
        shared[1],
        shared[2],
    )


def solution(mesh):
    in_specs = (
        P("dp", "tp", None),
        P("dp"),
        P("dp", None),
        P(),
        P(None, None, "tp"),
        P(None, "tp"),
        P("tp", None),
        P(),
        P(None, "tp"),
        P("tp"),
        P("tp", None),
        P(),
        P(),
        P("dp", "tp", None),
    )
    out_specs = (
        P("dp", "tp", None),
        P("dp", "tp", None),
        P(),
        P(None, None, "tp"),
        P(None, "tp"),
        P("tp", None),
        P(),
        P(None, "tp"),
        P("tp"),
        P("tp", None),
        P(),
        P(),
    )
    return jax.shard_map(shards, mesh=mesh, in_specs=in_specs, out_specs=out_specs, check_vma=False)
```

profile of v0, /device:TPU:0, one launch (start us, length us, event | category | flops | bytes accessed | tf_op | source)
XLA Modules:
  0.0 612.9 jit_solution(5548335376186596348)
XLA Ops:
  13.2 31.6 %all-gather.5.cloned.1.call-done = bf16[4,896,512]{2,1,0:T(8,128)(2,1)} async-done(((bf16[4,224,512]{2,1,0:T(8,128)(2,1)}), bf16[4,896,512]{2,1,0:T(8,128)(2,1)}) %all-gather.5.cloned.1.call-update) | async-done | bytes 3670032 | tf_op jit(solution)/shard_map/all_gather | solution.py:202
  44.8 4.1 add_convert_fusion
  53.3 23.3 %while.22 = (s32[]{:T(128)}, bf16[4,896,128]{1,2,0:T(8,128)(2,1)}, f32[4,2,896]{2,1,0:T(2,128)S(1)}, bf16[4,896,128]{1,2,0:T(8,128)(2,1)S(1)}, f32[4,896]{1,0:T(...) while((s32[]{:T(128)}, bf16[4,896,128]{1,2,0:T(8,128)(2,1)}, ...), condition=%wide.region_3.4_spmd, body=%wide.region_0.3_spmd.sunk | while | flops 430423168 | bytes 22084720 | solution.py:96
  76.6 5.9 fusion.42
  83.3 64.9 %reduce-scatter.5.cloned.1.call-done = f32[4,224,512]{2,1,0:T(8,128)} async-done(((f32[4,896,512]{2,1,0:T(8,128)}), f32[4,224,512]{2,1,0:T(8,128)}) %reduce-scatter.5.cloned.1.call-update) | async-done | bytes 1835024 | tf_op jit(solution)/shard_map/reduce_scatter | solution.py:206
  152.6 31.1 %all-gather.7.cloned.1.call-done = bf16[4,896,512]{2,1,0:T(8,128)(2,1)} async-done(((bf16[4,224,512]{2,1,0:T(8,128)(2,1)}), bf16[4,896,512]{2,1,0:T(8,128)(2,1)}) %all-gather.7.cloned.1.call-update) | async-done | bytes 3670032 | tf_op jit(solution)/shard_map/all_gather | solution.py:211
  183.7 4.2 fusion.39
  190.9 4.4 convolution_convert_fusion.2
  195.5 41.3 %reduce-scatter.7.cloned.1.call-done = bf16[4,224,512]{2,1,0:T(8,128)(2,1)} async-done(((bf16[4,896,512]{2,1,0:T(8,128)(2,1)}), bf16[4,224,512]{2,1,0:T(8,128)(2,1)}) %reduce-scatter.7.cloned.1.call-update) | async-done | bytes 917520 | tf_op jit(solution)/shard_map/reduce_scatter | solution.py:213
  242.7 31.6 %all-gather.9.cloned.1.call-done = bf16[4,896,512]{2,1,0:T(8,128)(2,1)} async-done(((bf16[4,224,512]{2,1,0:T(8,128)(2,1)}), bf16[4,896,512]{2,1,0:T(8,128)(2,1)}) %all-gather.9.cloned.1.call-update) | async-done | bytes 3670032 | tf_op jit(solution)/shard_map/all_gather | solution.py:223
  274.3 9.2 %fusion.58 = (f32[512]{0:T(512)S(1)}, bf16[4,896,512]{2,1,0:T(8,128)(2,1)S(1)}) fusion(f32[4,896,512]{2,1,0:T(8,128)} %copy-done.5, f32[512]{0:T(512)S(1)} %convert_element_type.131, bf16[4,896,512]{2,1,0:T(8,128)(2,1)} %all-gather.9.cloned.1.call-done, bf16[512,512]{1,0:T(8,128)(2,1)S(1)} %copy-done), kind=kOutput, calls=%fused_computation.123 | convolution fusion | flops 1919417856 | bytes 15208448 | tf_op jit(solution)/shard_map/wvd,fd->wvf/dot_general | solution.py:144
  285.5 4.1 convolution_convert_fusion.1
  289.8 41.2 %reduce-scatter.9.cloned.1.call-done = bf16[4,224,512]{2,1,0:T(8,128)(2,1)} async-done(((bf16[4,896,512]{2,1,0:T(8,128)(2,1)}), bf16[4,224,512]{2,1,0:T(8,128)(2,1)}) %reduce-scatter.9.cloned.1.call-update) | async-done | bytes 917520 | tf_op jit(solution)/shard_map/reduce_scatter | solution.py:227
  331.0 3.0 multiply_reduce_fusion.2
  336.0 31.6 %all-gather.11.cloned.1.call-done = bf16[4,896,512]{2,1,0:T(8,128)(2,1)} async-done(((bf16[4,224,512]{2,1,0:T(8,128)(2,1)}), bf16[4,896,512]{2,1,0:T(8,128)(2,1)}) %all-gather.11.cloned.1.call-update) | async-done | bytes 3670032 | tf_op jit(solution)/shard_map/all_gather | solution.py:234
  367.6 3.1 convolution_convert_fusion.3
  370.8 44.7 %while.23 = (s32[]{:T(128)}, bf16[4,896,384]{1,2,0:T(8,128)(2,1)}, bf16[4,896,128]{1,2,0:T(8,128)(2,1)S(1)}, f32[4,896]{1,0:T(4,128)S(1)}, bf16[4,896,128]{1,2,0...) while((s32[]{:T(128)}, bf16[4,896,384]{1,2,0:T(8,128)(2,1)}, ...), condition=%wide.region_17.18_spmd, body=%wide.region_15.17_spmd.sunk | while | flops 1054325888 | bytes 54190204 | solution.py:115
  415.5 5.7 convolution_convert_fusion
  421.5 6.3 %fusion.31 = f32[512,512]{1,0:T(8,128)} fusion(bf16[4,896,512]{2,1,0:T(8,128)(2,1)} %all-gather.7.cloned.1.call-done, bf16[4,896,512]{2,1,0:T(8,128)(2,1)} %copy-done.9), kind=kOutput, calls=%fused_computation.78 | convolution fusion | flops 1879048192 | bytes 8388608 | tf_op jit(solution)/shard_map/wvd,wvf->df/dot_general | solution.py:148
  427.8 8.5 %convolution_bitcast_fusion = f32[512,512]{1,0:T(8,128)} fusion(bf16[4,896,512]{2,1,0:T(8,128)(2,1)S(1)} %copy-done.22, f32[4,896,512]{2,1,0:T(8,128)} %copy-done.5, f32[512]{0:T(512)S(1)} %convert_element_type.131), kind=kOutput, calls=%fused_computation.77 | convolution fusion | flops 1897398272 | bytes 12060672 | tf_op jit(solution)/shard_map/wvf,wvd->fd/dot_general | solution.py:143
  439.1 3.8 convolution_bitcast_fusion.1
  445.3 22.0 %all-reduce.1 = (f32[2,128]{1,0:T(2,128)}, f32[512]{0:T(512)}) all-reduce(f32[2,128]{1,0:T(2,128)S(1)} %pad_maximum_fusion.4, f32[512]{0:T(512)S(1)} %get-tuple-element.207), channel_id=1, replica_groups=mesh['dp'=8,'tp'=4] {'dp'}, use_global_device_ids=true, to_apply=%region_23.24 | all-reduce | flops 768 | bytes 6144 | tf_op jit(solution)/shard_map/psum | solution.py:246
  470.1 41.5 %all-reduce = (f32[4,512]{1,0:T(4,128)}, f32[2,512]{1,0:T(2,128)}, f32[2,512]{1,0:T(2,128)}, f32[2,512]{1,0:T(2,128)}) all-reduce(f32[4,512]{1,0:T(4,128)S(1)} %fusion.44, f32[2,512]{1,0:T(2,128)S(1)} %pad_maximum_fusion, f32[2,512]{1,0:T(2,128)S(1)} %pad_maximum_fusion.1, ...), channel_id=1, replica_groups=mesh['dp'=8,'tp'=4] {'dp','tp'}, use_global_device_ids=true, to_apply=%region_20.21 | all-reduce | flops 5120 | bytes 40960 | tf_op jit(solution)/shard_map/psum | solution.py:247
  511.6 87.5 %all-reduce.5.cloned.1.call-done = (f32[3,512,128]{2,1,0:T(8,128)}, f32[128,512]{1,0:T(8,128)}, f32[512,512]{1,0:T(8,128)}, f32[512,512]{1,0:T(8,128)}) async-done(((f32[3,512,128]{2,1,0:T(8,128)}, f32[128,512]{1,0:T(8,128)}, f32[512,512]{1,0:T(8,128)}, f32[512,512]{1,0:T(8,128)}), (f32[3,512,128]{2,1,0:T(8,128)}, f32[128,512]{1,0:T(8,128)}, f32[512,512]{1,0:T(8,128)}, ...) | async-done | bytes 3145744 | tf_op jit(solution)/shard_map/psum | solution.py:246
  (199 shorter events, 111.2 us)
Async XLA Ops:
  7.2 183.8 %copy-start = (bf16[512,512]{1,0:T(8,128)(2,1)S(1)}, bf16[512,512]{1,0:T(8,128)(2,1)}, u32[]{:S(2)}) copy-start(bf16[512,512]{1,0:T(8,128)(2,1)} %param.28) | copy-start | bytes 1572868
  7.2 37.6 %all-gather.5.cloned.1.call-start = ((), (), s32[]{:S(2)}) async-start(), calls=%async_computation.4 | async-start | bytes 4587520 | tf_op jit(solution)/shard_map/all_gather | solution.py:202
  10.5 137.7 %reduce-scatter.5.cloned.1.call-start = ((), (), s32[]{:S(2)}) async-start(), calls=%async_computation.5 | async-start | bytes 9175040 | tf_op jit(solution)/shard_map/reduce_scatter | solution.py:206
  12.4 36.5 %copy-start.15 = (bf16[3,512,128]{1,2,0:T(8,128)(2,1)}, bf16[3,512,128]{1,2,0:T(8,128)(2,1)S(1)}, u32[]{:S(2)}) copy-start(bf16[3,512,128]{1,2,0:T(8,128)(2,1)S(1)} %copy.45) | copy-start | bytes 1179652
  53.3 23.3 %copy-start.13 = (bf16[128,512]{1,0:T(8,128)(2,1)S(1)}, bf16[128,512]{1,0:T(8,128)(2,1)}, u32[]{:S(2)}) copy-start(bf16[128,512]{1,0:T(8,128)(2,1)} %param.24) | copy-start | bytes 393220
  76.6 6.0 copy-start.3
  76.6 6.0 copy-start.4
  82.6 101.2 %all-gather.7.cloned.1.call-start = ((), (), s32[]{:S(2)}) async-start(), calls=%async_computation.6 | async-start | bytes 4587520 | tf_op jit(solution)/shard_map/all_gather | solution.py:211
  152.1 84.7 %reduce-scatter.7.cloned.1.call-start = ((), (), s32[]{:S(2)}) async-start(), calls=%async_computation.7 | async-start | bytes 4587520 | tf_op jit(solution)/shard_map/reduce_scatter | solution.py:213
  195.4 79.0 %all-gather.9.cloned.1.call-start = ((), (), s32[]{:S(2)}) async-start(), calls=%async_computation.8 | async-start | bytes 4587520 | tf_op jit(solution)/shard_map/all_gather | solution.py:223
  242.7 88.3 %reduce-scatter.9.cloned.1.call-start = ((), (), s32[]{:S(2)}) async-start(), calls=%async_computation.9 | async-start | bytes 4587520 | tf_op jit(solution)/shard_map/reduce_scatter | solution.py:227
  274.3 11.1 %copy-start.14 = (bf16[512,512]{1,0:T(8,128)(2,1)S(1)}, bf16[512,512]{1,0:T(8,128)(2,1)}, u32[]{:S(2)}) copy-start(bf16[512,512]{1,0:T(8,128)(2,1)} %param.26) | copy-start | bytes 1572868
  289.6 78.0 %all-gather.11.cloned.1.call-start = ((), (), s32[]{:S(2)}) async-start(), calls=%async_computation.10 | async-start | bytes 4587520 | tf_op jit(solution)/shard_map/all_gather | solution.py:234
  331.0 3.0 copy-start.10
  336.0 131.3 %reduce-scatter.11.cloned.1.call-start = ((), (), s32[]{:S(2)}) async-start(), calls=%async_computation.11 | async-start | bytes 4587520 | tf_op jit(solution)/shard_map/reduce_scatter | solution.py:238
  370.8 44.7 %copy-start.16 = (bf16[3,512,128]{1,2,0:T(8,128)(2,1)S(1)}, bf16[3,512,128]{1,2,0:T(8,128)(2,1)}, u32[]{:S(2)}) copy-start(bf16[3,512,128]{1,2,0:T(8,128)(2,1)} %copy-done.15) | copy-start | bytes 1179652
  421.2 177.8 %all-reduce.5.cloned.1.call-start = ((), (), s32[]{:S(2)}) async-start(), calls=%async_computation.12 | async-start | bytes 6291456 | tf_op jit(solution)/shard_map/psum | solution.py:246
  421.5 6.4 %copy-start.22 = (bf16[4,896,512]{2,1,0:T(8,128)(2,1)S(1)}, bf16[4,896,512]{2,1,0:T(8,128)(2,1)}, u32[]{:S(2)}) copy-start(bf16[4,896,512]{2,1,0:T(8,128)(2,1)} %all-gather.9.cloned.1.call-done) | copy-start | bytes 11010052
  427.8 8.5 %copy-start.11 = (bf16[4,896,384]{1,2,0:T(8,128)(2,1)S(1)}, bf16[4,896,384]{1,2,0:T(8,128)(2,1)}, u32[]{:S(2)}) copy-start(bf16[4,896,384]{1,2,0:T(8,128)(2,1)} %get-tuple-element.94) | copy-start | bytes 8257540
  427.8 8.5 %copy-start.21 = (bf16[4,896,512]{2,1,0:T(8,128)(2,1)S(1)}, bf16[4,896,512]{2,1,0:T(8,128)(2,1)}, u32[]{:S(2)}) copy-start(bf16[4,896,512]{2,1,0:T(8,128)(2,1)} %all-gather.5.cloned.1.call-done) | copy-start | bytes 11010052
  442.8 24.4 %copy-start.6 = (f32[4,224,512]{2,1,0:T(8,128)S(1)}, f32[4,224,512]{2,1,0:T(8,128)}, u32[]{:S(2)}) copy-start(f32[4,224,512]{2,1,0:T(8,128)} %get-tuple-element.177) | copy-start | bytes 5505028
  442.9 26.9 %copy-start.23 = (s32[4]{0:T(128)S(1)}, s32[4]{0:T(128)}, u32[]{:S(2)}) copy-start(s32[4]{0:T(128)} %param.19) | copy-start | bytes 52
  467.3 138.8 %copy-start.1 = (bf16[512,512]{1,0:T(8,128)(2,1)S(1)}, bf16[512,512]{1,0:T(8,128)(2,1)}, u32[]{:S(2)}) copy-start(bf16[512,512]{1,0:T(8,128)(2,1)} %param.28) | copy-start | bytes 1572868
  599.1 6.1 copy-start.12
  (9 other events, 17.3 us)
Sparse Core Ops, SparseCore 0:
  10.6 34.1 all-gather.4
  82.7 65.4 reduce-scatter.4
  152.2 31.4 all-gather.6
  195.5 41.2 reduce-scatter.6
  242.8 31.4 all-gather.8
  289.7 41.2 reduce-scatter.8
  336.1 31.5 all-gather.10
  421.3 41.2 reduce-scatter.10
  467.6 131.3 all-reduce.4
where the time goes:
time: 621 us; the launch traced here: 613 us
  waiting for transfers between devices  361 us (58%)
  matrix products  101 us (16%)
  blocking collectives  63.5 us (10%)
  other arithmetic  43.1 us (7%)
  local copies, waits for them, and re-layouts  27.7 us (4%)
  between operations  14.4 us (2%)
    psum x1, waiting for transfers between devices, shards(): lax.psum((qkv_grad, qvb_grad, out_grad, up_grad, upb_grad, down_grad), 'dp')  87.5 us
    reduce_scatter x1, waiting for transfers between devices, shards(): lax.psum_scatter(attn_part, 'tp', scatter_dimension=1, tiled=True)  64.9 us
    psum x1, blocking collectives, shards(): lax.psum((bias_grad, jnp.stack([gain_one, gain_two]), jnp.stack([shift_on...  41.5 us
    reduce_scatter x1, waiting for transfers between devices, shards(): lax.psum_scatter(ffn_part.astype(jnp.bfloat16), 'tp', scatter_dimension=1...  41.3 us
    reduce_scatter x1, waiting for transfers between devices, shards(): lax.psum_scatter(ffn_back_part.astype(jnp.bfloat16), 'tp', scatter_dimens...  41.2 us
    all_gather x1, waiting for transfers between devices, shards(): act_full = lax.all_gather(act_in, 'tp', axis=1, tiled=True)  31.6 us
    all_gather x1, waiting for transfers between devices, shards(): grad_two_full = lax.all_gather(grad_two_low, 'tp', axis=1, tiled=True)  31.6 us
    all_gather x1, waiting for transfers between devices, shards(): grad_one_full = lax.all_gather(grad_one_low, 'tp', axis=1, tiled=True)  31.6 us
  transfers between devices with their start and end apart: 9, of which 8 were waited for; matrix products, arithmetic and copies ran while one was open for 5% of the time, Pallas kernels for 0%

commit v1 on v0

--- a/solution.py
+++ b/solution.py
@@ -245,13 +245,16 @@
     qvb_grad = jnp.stack([bcat_grad[:col_width], bcat_grad[2 * col_width :]])
     weight_totals = lax.psum((qkv_grad, qvb_grad, out_grad, up_grad, upb_grad, down_grad), "dp")
     shared = lax.psum(
-        (
-            bias_grad,
-            jnp.stack([gain_one, gain_two]),
-            jnp.stack([shift_one, shift_two]),
-            jnp.stack([jnp.sum(grad_one, axis=(0, 1)), jnp.sum(grad_two, axis=(0, 1))]),
+        lax.psum(
+            (
+                bias_grad,
+                jnp.stack([gain_one, gain_two]),
+                jnp.stack([shift_one, shift_two]),
+                jnp.stack([jnp.sum(grad_one, axis=(0, 1)), jnp.sum(grad_two, axis=(0, 1))]),
+            ),
+            "tp",
         ),
-        ("dp", "tp"),
+        "dp",
     )
     return (
         result_rows,

time: 621 us -> 647 us (1.042)
  matrix products: 101 us -> 126 us
  blocking collectives: 63.5 us -> 49.9 us
  waiting for transfers between devices: 361 us -> 373 us
    psum x1, blocking collectives: 41.5 us -> 10.3 us  [shards(): lax.psum((bias_grad, jnp.stack([gain_one, gain_two]), jnp.stack([shift_on...]
    psum x1, blocking collectives: 22 us -> 39.6 us  [shards(): lax.psum(lax.psum((bias_grad, jnp.stack([gain_one, gain_two]), jnp.stack(...]
    reduce_scatter x1, waiting for transfers between devices: 0.01 us -> 15.8 us  [shards(): lax.psum_scatter(attn_back_part.astype(jnp.bfloat16), 'tp', scatter_dimen...]
    dot_general x4, matrix products: 8.49 us -> 20.3 us  [attend_back(): jnp.einsum('qhe,khe->hqk', grad_heads, v_heads, preferred_element_type=jn...]
    dot_general x8, matrix products: 9.59 us -> 20.5 us  [masked_scores(): jnp.einsum('qhe,khe->hqk', q_heads, k_heads, preferred_element_type=jnp.f...]
    unnamed x53 -> x47, local copies, waits for them, and re-layouts: 13.7 us -> 13.8 us
  transfers between devices with their start and end apart: 9 -> 9, of which waited for: 8 -> 9; matrix products, arithmetic and copies ran while one was open for 5% -> 5% of each run, Pallas kernels for 0% -> 0%
where the time goes in v1:
time: 647 us; the launch traced here: 639 us
  waiting for transfers between devices  373 us (58%)
  matrix products  126 us (19%)
  blocking collectives  49.9 us (8%)
  other arithmetic  43.2 us (7%)
  local copies, waits for them, and re-layouts  31 us (5%)
  between operations  14.4 us (2%)
    psum x1, waiting for transfers between devices, shards(): lax.psum((qkv_grad, qvb_grad, out_grad, up_grad, upb_grad, down_grad), 'dp')  83.2 us
    reduce_scatter x1, waiting for transfers between devices, shards(): lax.psum_scatter(attn_part, 'tp', scatter_dimension=1, tiled=True)  64.9 us
    reduce_scatter x1, waiting for transfers between devices, shards(): lax.psum_scatter(ffn_part.astype(jnp.bfloat16), 'tp', scatter_dimension=1...  41.3 us
    reduce_scatter x1, waiting for transfers between devices, shards(): lax.psum_scatter(ffn_back_part.astype(jnp.bfloat16), 'tp', scatter_dimens...  41.2 us
    psum x1, blocking collectives, shards(): lax.psum(lax.psum((bias_grad, jnp.stack([gain_one, gain_two]), jnp.stack(...  39.6 us
    all_gather x1, waiting for transfers between devices, shards(): grad_two_full = lax.all_gather(grad_two_low, 'tp', axis=1, tiled=True)  31.6 us
    all_gather x1, waiting for transfers between devices, shards(): act_full = lax.all_gather(act_in, 'tp', axis=1, tiled=True)  31.6 us
    all_gather x1, waiting for transfers between devices, shards(): grad_one_full = lax.all_gather(grad_one_low, 'tp', axis=1, tiled=True)  31.6 us
  transfers between devices with their start and end apart: 9, of which 9 were waited for; matrix products, arithmetic and copies ran while one was open for 5% of the time, Pallas kernels for 0%

profile of v1, /device:TPU:0, one launch (start us, length us, event | category | flops | bytes accessed | tf_op | source)
XLA Modules:
  0.0 638.8 jit_solution(702686491584198822)
XLA Ops:
  13.2 31.6 %all-gather.5.cloned.1.call-done = bf16[4,896,512]{2,1,0:T(8,128)(2,1)} async-done(((bf16[4,224,512]{2,1,0:T(8,128)(2,1)}), bf16[4,896,512]{2,1,0:T(8,128)(2,1)}) %all-gather.5.cloned.1.call-update) | async-done | bytes 3670032 | tf_op jit(solution)/shard_map/all_gather | solution.py:202
  53.3 23.2 %while.22 = (s32[]{:T(128)}, bf16[4,896,128]{1,2,0:T(8,128)(2,1)}, f32[4,2,896]{2,1,0:T(2,128)S(1)}, bf16[4,896,128]{1,2,0:T(8,128)(2,1)S(1)}, f32[4,896]{1,0:T(...) while((s32[]{:T(128)}, bf16[4,896,128]{1,2,0:T(8,128)(2,1)}, ...), condition=%wide.region_3.4_spmd, body=%wide.region_0.3_spmd.sunk | while | flops 430423168 | bytes 22085220 | solution.py:96
  76.6 5.9 fusion.42
  83.3 64.9 %reduce-scatter.5.cloned.1.call-done = f32[4,224,512]{2,1,0:T(8,128)} async-done(((f32[4,896,512]{2,1,0:T(8,128)}), f32[4,224,512]{2,1,0:T(8,128)}) %reduce-scatter.5.cloned.1.call-update) | async-done | bytes 1835024 | tf_op jit(solution)/shard_map/reduce_scatter | solution.py:206
  152.6 31.1 %all-gather.7.cloned.1.call-done = bf16[4,896,512]{2,1,0:T(8,128)(2,1)} async-done(((bf16[4,224,512]{2,1,0:T(8,128)(2,1)}), bf16[4,896,512]{2,1,0:T(8,128)(2,1)}) %all-gather.7.cloned.1.call-update) | async-done | bytes 3670032 | tf_op jit(solution)/shard_map/all_gather | solution.py:211
  183.7 4.2 fusion.39
  190.9 4.4 convolution_convert_fusion.2
  195.5 41.3 %reduce-scatter.7.cloned.1.call-done = bf16[4,224,512]{2,1,0:T(8,128)(2,1)} async-done(((bf16[4,896,512]{2,1,0:T(8,128)(2,1)}), bf16[4,224,512]{2,1,0:T(8,128)(2,1)}) %reduce-scatter.7.cloned.1.call-update) | async-done | bytes 917520 | tf_op jit(solution)/shard_map/reduce_scatter | solution.py:213
  242.8 31.6 %all-gather.9.cloned.1.call-done = bf16[4,896,512]{2,1,0:T(8,128)(2,1)} async-done(((bf16[4,224,512]{2,1,0:T(8,128)(2,1)}), bf16[4,896,512]{2,1,0:T(8,128)(2,1)}) %all-gather.9.cloned.1.call-update) | async-done | bytes 3670032 | tf_op jit(solution)/shard_map/all_gather | solution.py:223
  274.4 9.3 %fusion.58 = (f32[512]{0:T(512)S(1)}, bf16[4,896,512]{2,1,0:T(8,128)(2,1)S(1)}) fusion(f32[4,896,512]{2,1,0:T(8,128)} %copy-done.5, f32[512]{0:T(512)S(1)} %convert_element_type.131, bf16[4,896,512]{2,1,0:T(8,128)(2,1)} %all-gather.9.cloned.1.call-done, bf16[512,512]{1,0:T(8,128)(2,1)S(1)} %copy-done), kind=kOutput, calls=%fused_computation.123 | convolution fusion | flops 1919417856 | bytes 15208448 | tf_op jit(solution)/shard_map/wvd,fd->wvf/dot_general | solution.py:144
  290.0 41.2 %reduce-scatter.9.cloned.1.call-done = bf16[4,224,512]{2,1,0:T(8,128)(2,1)} async-done(((bf16[4,896,512]{2,1,0:T(8,128)(2,1)}), bf16[4,224,512]{2,1,0:T(8,128)(2,1)}) %reduce-scatter.9.cloned.1.call-update) | async-done | bytes 917520 | tf_op jit(solution)/shard_map/reduce_scatter | solution.py:227
  336.2 31.6 %all-gather.11.cloned.1.call-done = bf16[4,896,512]{2,1,0:T(8,128)(2,1)} async-done(((bf16[4,224,512]{2,1,0:T(8,128)(2,1)}), bf16[4,896,512]{2,1,0:T(8,128)(2,1)}) %all-gather.11.cloned.1.call-update) | async-done | bytes 3670032 | tf_op jit(solution)/shard_map/all_gather | solution.py:234
  370.9 70.9 %while.23 = (s32[]{:T(128)}, bf16[4,896,384]{1,2,0:T(8,128)(2,1)}, bf16[4,896,128]{1,2,0:T(8,128)(2,1)}, f32[4,896]{1,0:T(4,128)S(1)}, bf16[4,896,128]{1,2,0:T(8...) while((s32[]{:T(128)}, bf16[4,896,384]{1,2,0:T(8,128)(2,1)}, ...), condition=%wide.region_17.18_spmd, body=%wide.region_15.17_spmd.sunk | while | flops 1054325888 | bytes 73458336 | solution.py:115
  376.9 5.1 multiply_reduce_fusion.9
  394.7 5.1 multiply_reduce_fusion.9
  412.4 5.1 multiply_reduce_fusion.9
  430.1 5.1 multiply_reduce_fusion.9
  441.9 5.8 convolution_convert_fusion
  448.0 6.3 fusion.31
  454.4 8.4 %convolution_bitcast_fusion = f32[512,512]{1,0:T(8,128)} fusion(bf16[4,896,512]{2,1,0:T(8,128)(2,1)S(1)} %copy-done.19, f32[4,896,512]{2,1,0:T(8,128)} %copy-done.5, f32[512]{0:T(512)S(1)} %convert_element_type.131), kind=kOutput, calls=%fused_computation.77 | convolution fusion | flops 1897398272 | bytes 12060672 | tf_op jit(solution)/shard_map/wvf,wvd->fd/dot_general | solution.py:143
  473.4 15.8 %reduce-scatter.11.cloned.1.call-done = bf16[4,224,512]{2,1,0:T(8,128)(2,1)} async-done(((bf16[4,896,512]{2,1,0:T(8,128)(2,1)}), bf16[4,224,512]{2,1,0:T(8,128)(2,1)}) %reduce-scatter.11.cloned.1.call-update) | async-done | bytes 917520 | tf_op jit(solution)/shard_map/reduce_scatter | solution.py:238
  491.9 10.3 %all-reduce.2 = (f32[4,512]{1,0:T(4,128)S(1)}, f32[2,512]{1,0:T(2,128)S(1)}, f32[2,512]{1,0:T(2,128)S(1)}, f32[2,512]{1,0:T(2,128)S(1)}) all-reduce(f32[4,512]{1,0:T(4,128)S(1)} %fusion.44, f32[2,512]{1,0:T(2,128)S(1)} %pad_maximum_fusion, f32[2,512]{1,0:T(2,128)S(1)} %pad_maximum_fusion.1, ...), channel_id=1, replica_groups=mesh['dp'=8,'tp'=4] {'tp'}, use_global_device_ids=true, to_apply=%region_20.21 | all-reduce | flops 5120 | bytes 40960 | tf_op jit(solution)/shard_map/psum | solution.py:248
  502.2 39.6 %all-reduce = (f32[4,512]{1,0:T(4,128)}, f32[2,128]{1,0:T(2,128)}, f32[2,512]{1,0:T(2,128)}, f32[512]{0:T(512)}, f32[2,512]{1,0:T(2,128)}, /*index=5*/f32[2,512]{1,0:T(2,128)}) all-reduce(f32[4,512]{1,0:T(4,128)S(1)} %get-tuple-element.176, f32[2,128]{1,0:T(2,128)S(1)} %pad_maximum_fusion.4, ...), channel_id=1, replica_groups=mesh['dp'=8,'tp'=4] {'dp'}, use_global_device_ids=true, to_apply=%region_21.22 | all-reduce | flops 5888 | bytes 47104 | tf_op jit(solution)/shard_map/psum | solution.py:247
  541.8 83.2 %all-reduce.5.cloned.1.call-done = (f32[3,512,128]{2,1,0:T(8,128)}, f32[128,512]{1,0:T(8,128)}, f32[512,512]{1,0:T(8,128)}, f32[512,512]{1,0:T(8,128)}) async-done(((f32[3,512,128]{2,1,0:T(8,128)}, f32[128,512]{1,0:T(8,128)}, f32[512,512]{1,0:T(8,128)}, f32[512,512]{1,0:T(8,128)}), (f32[3,512,128]{2,1,0:T(8,128)}, f32[128,512]{1,0:T(8,128)}, f32[512,512]{1,0:T(8,128)}, ...) | async-done | bytes 3145744 | tf_op jit(solution)/shard_map/psum | solution.py:246
  (213 shorter events, 137.0 us)
Async XLA Ops:
  7.2 183.7 %copy-start = (bf16[512,512]{1,0:T(8,128)(2,1)S(1)}, bf16[512,512]{1,0:T(8,128)(2,1)}, u32[]{:S(2)}) copy-start(bf16[512,512]{1,0:T(8,128)(2,1)} %param.28) | copy-start | bytes 1572868
  7.2 37.6 %all-gather.5.cloned.1.call-start = ((), (), s32[]{:S(2)}) async-start(), calls=%async_computation.4 | async-start | bytes 4587520 | tf_op jit(solution)/shard_map/all_gather | solution.py:202
  10.5 137.7 %reduce-scatter.5.cloned.1.call-start = ((), (), s32[]{:S(2)}) async-start(), calls=%async_computation.5 | async-start | bytes 9175040 | tf_op jit(solution)/shard_map/reduce_scatter | solution.py:206
  11.7 33.1 %copy-start.13 = (bf16[3,512,128]{1,2,0:T(8,128)(2,1)}, bf16[3,512,128]{1,2,0:T(8,128)(2,1)S(1)}, u32[]{:S(2)}) copy-start(bf16[3,512,128]{1,2,0:T(8,128)(2,1)S(1)} %copy.45) | copy-start | bytes 1179652
  53.3 23.3 %copy-start.11 = (bf16[128,512]{1,0:T(8,128)(2,1)S(1)}, bf16[128,512]{1,0:T(8,128)(2,1)}, u32[]{:S(2)}) copy-start(bf16[128,512]{1,0:T(8,128)(2,1)} %param.24) | copy-start | bytes 393220
  76.6 6.0 copy-start.3
  76.6 6.0 copy-start.4
  82.6 101.2 %all-gather.7.cloned.1.call-start = ((), (), s32[]{:S(2)}) async-start(), calls=%async_computation.6 | async-start | bytes 4587520 | tf_op jit(solution)/shard_map/all_gather | solution.py:211
  152.1 84.7 %reduce-scatter.7.cloned.1.call-start = ((), (), s32[]{:S(2)}) async-start(), calls=%async_computation.7 | async-start | bytes 4587520 | tf_op jit(solution)/shard_map/reduce_scatter | solution.py:213
  195.4 79.0 %all-gather.9.cloned.1.call-start = ((), (), s32[]{:S(2)}) async-start(), calls=%async_computation.8 | async-start | bytes 4587520 | tf_op jit(solution)/shard_map/all_gather | solution.py:223
  242.7 88.5 %reduce-scatter.9.cloned.1.call-start = ((), (), s32[]{:S(2)}) async-start(), calls=%async_computation.9 | async-start | bytes 4587520 | tf_op jit(solution)/shard_map/reduce_scatter | solution.py:227
  274.4 11.2 %copy-start.12 = (bf16[512,512]{1,0:T(8,128)(2,1)S(1)}, bf16[512,512]{1,0:T(8,128)(2,1)}, u32[]{:S(2)}) copy-start(bf16[512,512]{1,0:T(8,128)(2,1)} %param.26) | copy-start | bytes 1572868
  289.7 78.0 %all-gather.11.cloned.1.call-start = ((), (), s32[]{:S(2)}) async-start(), calls=%async_computation.10 | async-start | bytes 4587520 | tf_op jit(solution)/shard_map/all_gather | solution.py:234
  336.1 153.0 %reduce-scatter.11.cloned.1.call-start = ((), (), s32[]{:S(2)}) async-start(), calls=%async_computation.11 | async-start | bytes 4587520 | tf_op jit(solution)/shard_map/reduce_scatter | solution.py:238
  376.9 5.1 slice-start
  394.6 5.1 slice-start
  412.4 5.1 slice-start
  447.7 177.3 %all-reduce.5.cloned.1.call-start = ((), (), s32[]{:S(2)}) async-start(), calls=%async_computation.12 | async-start | bytes 6291456 | tf_op jit(solution)/shard_map/psum | solution.py:246
  448.0 6.4 copy-start.19
  454.4 8.4 %copy-start.18 = (bf16[4,896,512]{2,1,0:T(8,128)(2,1)S(1)}, bf16[4,896,512]{2,1,0:T(8,128)(2,1)}, u32[]{:S(2)}) copy-start(bf16[4,896,512]{2,1,0:T(8,128)(2,1)} %all-gather.5.cloned.1.call-done) | copy-start | bytes 11010052
  470.9 18.2 %copy-start.6 = (f32[4,224,512]{2,1,0:T(8,128)S(1)}, f32[4,224,512]{2,1,0:T(8,128)}, u32[]{:S(2)}) copy-start(f32[4,224,512]{2,1,0:T(8,128)} %get-tuple-element.181) | copy-start | bytes 5505028
  470.9 20.7 %copy-start.20 = (s32[4]{0:T(128)S(1)}, s32[4]{0:T(128)}, u32[]{:S(2)}) copy-start(s32[4]{0:T(128)} %param.19) | copy-start | bytes 52
  489.1 142.9 %copy-start.1 = (bf16[512,512]{1,0:T(8,128)(2,1)S(1)}, bf16[512,512]{1,0:T(8,128)(2,1)}, u32[]{:S(2)}) copy-start(bf16[512,512]{1,0:T(8,128)(2,1)} %param.28) | copy-start | bytes 1572868
  625.0 6.1 copy-start.10
  (14 other events, 43.2 us)
Sparse Core Ops, SparseCore 0:
  10.6 34.1 all-gather.4
  82.7 65.4 reduce-scatter.4
  152.2 31.4 all-gather.6
  195.5 41.2 reduce-scatter.6
  242.8 31.4 all-gather.8
  289.9 41.2 reduce-scatter.8
  336.2 31.4 all-gather.10
  447.9 41.2 reduce-scatter.10
  494.2 130.7 all-reduce.4
